TPU v7x, 32 devices: a whole 2x2x4 slice. The times are simulated.
32 devices in a mesh: pipe: 4 (over x, core), dp: 2 (over y), tensor: 4 (over z).
Axes of the slice: x: 2, y: 2, z: 4, core: 2. Of those that a mesh axis runs over, the one named last changes fastest.
Arguments:
- section_input: bfloat16 [4, 128, 8192], P('pipe', 'dp'), may hold values from -6 to 6
- norm_gain: float32 [4, 8192], P('pipe'), may hold values from 0.1 to 1.9
- projection: bfloat16 [4, 8192, 4096], P('pipe', 'dp', 'tensor'), may hold values from -0.0625 to 0.0625
- upstream_grad: bfloat16 [4, 128, 4096], P('pipe', 'dp', 'tensor'), may hold values from -4 to 4
Outputs:
- shifted_output: bfloat16 [4, 128, 4096], P('pipe', 'dp', 'tensor')
- normed_grad: bfloat16 [4, 128, 8192], P('pipe', None, ('dp', 'tensor'))
All inputs are finite; a program needn't handle non-finite values.
Results may differ from a plain program's by a relative error of at most 0.013.
Values may be sent and summed in bfloat16 or wider, within the bound.
A program may use at most 64 MiB of HBM per device.

v0:
```python
import jax
import jax.numpy as jnp
from jax import lax
from jax.sharding import PartitionSpec as P


def passed_along(block, axis, distance):
    devices = range(lax.axis_size(axis))
    route = [((i - distance) % len(devices), i) for i in devices]
    return lax.ppermute(block, axis, route)


def per_device(section_input, norm_gain, projection, upstream_grad):
    section_x = section_input[0]
    weight = projection[0]
    cot = upstream_grad[0]
    out_cols = weight.shape[1]
    xf = section_x.astype(jnp.float32)
    meansq = jnp.mean(xf * xf, axis=-1, keepdims=True)
    normed = (xf * lax.rsqrt(meansq + 1e-05) * norm_gain[0]).astype(jnp.bfloat16)
    features = lax.all_to_all(normed, "dp", split_axis=1, concat_axis=0, tiled=True)
    residual = lax.dynamic_slice_in_dim(xf, lax.axis_index("tensor") * out_cols, out_cols, 1)
    pre = lax.psum_scatter(
        jnp.dot(features, weight, preferred_element_type=jnp.float32).astype(jnp.bfloat16),
        "dp",
        scatter_dimension=0,
        tiled=True,
    ).astype(jnp.float32)
    act, back = jax.vjp(jax.nn.gelu, pre)
    pre_grad = back(cot.astype(jnp.float32))[0].astype(jnp.bfloat16)
    grad_all = lax.all_gather(pre_grad, "dp", axis=0, tiled=True)
    layer_out = (residual + act).astype(jnp.bfloat16)
    shifted = passed_along(layer_out, "pipe", 1)
    partial_grad = lax.dot_general(
        grad_all, weight, (((1,), (1,)), ((), ())), preferred_element_type=jnp.float32
    )
    normed_grad = lax.psum_scatter(
        partial_grad.astype(jnp.bfloat16), "tensor", scatter_dimension=1, tiled=True
    )
    return (shifted[None], normed_grad[None])


def solution(mesh):
    in_specs = (
        P("pipe", "dp", None),
        P("pipe", None),
        P("pipe", "dp", "tensor"),
        P("pipe", "dp", "tensor"),
    )
    out_specs = (P("pipe", "dp", "tensor"), P("pipe", None, ("dp", "tensor")))
    return jax.shard_map(
        per_device, mesh=mesh, in_specs=in_specs, out_specs=out_specs, check_vma=False
    )
```

profile of v0, /device:TPU:0, one launch (start us, length us, event | category | flops | bytes accessed | tf_op | source)
XLA Modules:
  0.0 98.4 jit_solution(15444062869844749553)
XLA Ops:
  7.2 0.0 copy-start
  7.2 0.0 copy-start.2
  7.2 0.0 reduce-scatter.3.cloned.1.call-start
  7.2 3.2 %reshape.33 = f32[64,2,4096]{2,1,0:T(2,128)S(1)} reshape(bf16[1,64,8192]{2,1,0:T(8,128)(2,1)} %param.4) | data formatting | bytes 3145728 | tf_op jit(solution)/shard_map/convert_element_type | solution.py:18
  10.4 0.0 copy-done
  10.5 0.3 multiply_reduce_fusion
  10.8 0.5 broadcast.45
  11.3 0.0 copy-done.2
  11.3 0.7 reduce.4
  12.0 1.3 %multiply_convert_fusion = bf16[64,2,4096]{2,1,0:T(2,128)(2,1)S(1)} fusion(f32[64,2,4096]{2,1,0:T(2,128)S(1)} %reshape.33, f32[64]{0:T(128)S(1)} %add_rsqrt_fusion, f32[2,4096]{1,0:T(2,128)S(1)} %mul.75), kind=kLoop, calls=%fused_computation.5 | loop fusion | flops 1572864 | bytes 3178752 | tf_op jit(solution)/shard_map/convert_element_type | solution.py:20
  13.4 0.6 copy.7
  14.0 17.6 %all_to_all.16 = bf16[64,2,4096]{2,0,1:T(8,128)(2,1)S(1)} all-to-all(bf16[64,2,4096]{2,0,1:T(8,128)(2,1)S(1)} %copy.7), channel_id=1, replica_groups=mesh['pipe'=4,'dp'=2,'tensor'=4] {'dp'}, dimensions={1} | all-to-all | bytes 2097152 | tf_op jit(solution)/shard_map/all_to_all | solution.py:21
  31.6 5.4 %fusion.7 = bf16[128,1024]{1,0:T(8,128)(2,1)} fusion(bf16[128,4096]{1,0:T(8,128)(2,1)S(1)} %bitcast.21, bf16[1,4096,1024]{2,1,0:T(8,128)(2,1)} %param.6), kind=kOutput, calls=%fused_computation.7 | convolution fusion | flops 1073872896 | bytes 9699328 | tf_op jit(solution)/shard_map/dot_general | solution.py:24
  37.0 0.0 copy-start.1
  37.0 0.0 reduce-scatter.3.cloned.1.call-update
  37.0 0.0 reduce-scatter.5.cloned.1.call-start
  37.1 0.1 convert_element_type.35
  37.2 12.1 %reduce-scatter.3.cloned.1.call-done = bf16[64,1024]{1,0:T(8,128)(2,1)} async-done(((bf16[128,1024]{1,0:T(8,128)(2,1)}), bf16[64,1024]{1,0:T(8,128)(2,1)}) %reduce-scatter.3.cloned.1.call-update) | async-done | bytes 131088 | tf_op jit(solution)/shard_map/reduce_scatter | solution.py:23
  49.3 0.0 copy-done.1
  49.3 1.1 %fusion.13 = (bf16[64,1024]{1,0:T(8,128)(2,1)S(1)}, bf16[64,1024]{1,0:T(8,128)(2,1)S(1)}) fusion(bf16[64,1024]{1,0:T(8,128)(2,1)} %reduce-scatter.3.cloned.1.call-done, bf16[1,64,1024]{2,1,0:T(8,128)(2,1)S(1)} %copy-done.1, f32[1,64,8192]{2,1,0:T(8,128)S(1)} %convert_element_type.35, s32[]{:T(128)S(6)} %select_n.3), kind=kLoop, calls=%fused_computation.17 | loop fusion | flops 1638400 | bytes 786436 | tf_op jit(solution)/shard_map/convert_element_type | solution.py:30
  50.4 5.9 %all_gather.3 = bf16[128,1024]{1,0:T(8,128)(2,1)S(1)} all-gather(bf16[64,1024]{1,0:T(8,128)(2,1)S(1)} %get-tuple-element.2), channel_id=1, replica_groups=mesh['pipe'=4,'dp'=2,'tensor'=4] {'dp'}, dimensions={0}, use_global_device_ids=true | all-gather | bytes 393216 | tf_op jit(solution)/shard_map/all_gather | solution.py:31
  56.4 7.3 %fusion.4 = bf16[128,4096]{1,0:T(8,128)(2,1)} fusion(bf16[128,1024]{1,0:T(8,128)(2,1)S(1)} %all_gather.3, bf16[1,4096,1024]{2,1,0:T(8,128)(2,1)} %param.6), kind=kOutput, calls=%fused_computation.4 | convolution fusion | flops 1074266112 | bytes 9699328 | tf_op jit(solution)/shard_map/dot_general | solution.py:34
  63.6 0.0 reduce-scatter.5.cloned.1.call-update
  63.6 0.1 collective-permute-start
  63.7 4.4 %collective-permute-done = bf16[64,1024]{1,0:T(8,128)(2,1)S(1)} collective-permute-done((bf16[64,1024]{1,0:T(8,128)(2,1)S(1)}, bf16[64,1024]{1,0:T(8,128)(2,1)S(1)}, u32[]{:S(2)}, u32[]{:S(2)}) %collective-permute-start) | collective-permute-done | bytes 131104 | tf_op jit(solution)/shard_map/ppermute | solution.py:10
  68.1 22.8 %reduce-scatter.5.cloned.1.call-done = bf16[128,1024]{1,0:T(8,128)(2,1)} async-done(((bf16[128,4096]{1,0:T(8,128)(2,1)}), bf16[128,1024]{1,0:T(8,128)(2,1)}) %reduce-scatter.5.cloned.1.call-update) | async-done | bytes 262160 | tf_op jit(solution)/shard_map/reduce_scatter | solution.py:37
  90.9 0.7 copy.9
  (2 shorter events, 0.0 us)
Async XLA Ops:
  7.2 3.3 %copy-start = (bf16[1,64,8192]{2,1,0:T(8,128)(2,1)S(1)}, bf16[1,64,8192]{2,1,0:T(8,128)(2,1)}, u32[]{:S(2)}) copy-start(bf16[1,64,8192]{2,1,0:T(8,128)(2,1)} %param.4) | copy-start | bytes 3145732
  7.2 4.1 %copy-start.2 = (f32[1,8192]{1,0:T(1,128)S(1)}, f32[1,8192]{1,0:T(1,128)}, u32[]{:S(2)}) copy-start(f32[1,8192]{1,0:T(1,128)} %param.5) | copy-start | bytes 98308
  7.2 42.1 %reduce-scatter.3.cloned.1.call-start = ((), (), s32[]{:S(2)}) async-start(), calls=%async_computation.3 | async-start | bytes 393216 | tf_op jit(solution)/shard_map/reduce_scatter | solution.py:23
  37.0 12.3 %copy-start.1 = (bf16[1,64,1024]{2,1,0:T(8,128)(2,1)S(1)}, bf16[1,64,1024]{2,1,0:T(8,128)(2,1)}, u32[]{:S(2)}) copy-start(bf16[1,64,1024]{2,1,0:T(8,128)(2,1)} %param.7) | copy-start | bytes 393220
  37.0 53.9 %reduce-scatter.5.cloned.1.call-start = ((), (), s32[]{:S(2)}) async-start(), calls=%async_computation.4 | async-start | bytes 1310720 | tf_op jit(solution)/shard_map/reduce_scatter | solution.py:37
  63.6 4.4 %collective-permute-start = (bf16[64,1024]{1,0:T(8,128)(2,1)S(1)}, bf16[64,1024]{1,0:T(8,128)(2,1)S(1)}, u32[]{:S(2)}, u32[]{:S(2)}) collective-permute-start(bf16[64,1024]{1,0:T(8,128)(2,1)S(1)} %get-tuple-element.3), channel_id=1, source_target_pairs={{24,0},{0,8},{8,16},{16,24},{25,1},{1,9},{9,17},{17,25},{26,2},{2,... | collective-permute-start | bytes 393224 | tf_op jit(solution)/shard_map/ppermute | solution.py:10
Sparse Core Ops, SparseCore 0:
  37.2 12.0 reduce-scatter.2
  63.8 27.1 reduce-scatter.4
where the time goes:
time: 98.7 us; the launch traced here: 98.4 us
  waiting for transfers between devices  39.3 us (40%)
  blocking collectives  23.6 us (24%)
  between operations  14.1 us (14%)
  matrix products  12.7 us (13%)
  local copies, waits for them, and re-layouts  5 us (5%)
  other arithmetic  3.62 us (4%)
    reduce_scatter x1, waiting for transfers between devices, per_device(): lax.psum_scatter(partial_grad.astype(jnp.bfloat16), 'tensor', scatter_dim...  22.8 us
    all_to_all x1, blocking collectives, per_device(): lax.all_to_all(normed, 'dp', split_axis=1, concat_axis=0, tiled=True)  17.6 us
    reduce_scatter x1, waiting for transfers between devices, per_device(): lax.psum_scatter(jnp.dot(features, weight, preferred_element_type=jnp.flo...  12.1 us
    dot_general x1, matrix products, per_device(): lax.dot_general(grad_all, weight, (((1,), (1,)), ((), ())), preferred_ele...  7.26 us
    all_gather x1, blocking collectives, per_device(): grad_all = lax.all_gather(pre_grad, 'dp', axis=0, tiled=True)  5.93 us
    dot_general x1, matrix products, per_device(): jnp.dot(features, weight, preferred_element_type=jnp.float32)  5.42 us
    ppermute x1, waiting for transfers between devices, passed_along(): return lax.ppermute(block, axis, route)  4.38 us
    convert_element_type x1, local copies, waits for them, and re-layouts, per_device(): xf = section_x.astype(jnp.float32)  3.21 us
  transfers between devices with their start and end apart: 3, of which 3 were waited for; matrix products, arithmetic and copies ran while one was open for 0% of the time, Pallas kernels for 0%

commit v1 on v0

v1 whole, which is shorter than its diff:
```python
import functools

import jax
import jax.numpy as jnp
from jax import lax
from jax.experimental import pallas as pl
from jax.experimental.pallas import tpu as pltpu
from jax.sharding import PartitionSpec as P

F32 = jnp.float32
BF16 = jnp.bfloat16
MESH = pl.DeviceIdType.MESH
NS = 4


def kernel(
    np_, nd, nt,
    x_ref, g_ref, w_ref, c_ref,
    sh_ref, ng_ref,
    xv, gv, wv, cv, rs, rsr, xr, acc, ps, pr, lo, pgv, pgr, gp, rb,
    lsem, wsem,
    st_s, st_r, x_s, x_r, p_s, p_r, g_s, g_r, sh_s, sh_r,
    a_s, a_r, r_s, r_r, c_s, c_r,
):
    p = lax.axis_index("pipe")
    d = lax.axis_index("dp")
    t = lax.axis_index("tensor")
    T, D = x_ref.shape[1], x_ref.shape[2]
    K, C = w_ref.shape[1], w_ref.shape[2]
    KC, KQ = K // NS, K // nt

    def remote(src, dst, ss, rsem, **dev):
        return pltpu.make_async_remote_copy(
            src_ref=src, dst_ref=dst, send_sem=ss, recv_sem=rsem,
            device_id=dev, device_id_type=MESH,
        )

    nxt, prv = lax.rem(p + 1, np_), lax.rem(p + np_ - 1, np_)
    barrier = pltpu.get_barrier_semaphore()
    for o in range(1, nd):
        pl.semaphore_signal(barrier, inc=1, device_id={"dp": lax.rem(d + o, nd)}, device_id_type=MESH)
    for o in range(1, nt):
        pl.semaphore_signal(barrier, inc=1, device_id={"tensor": lax.rem(t + o, nt)}, device_id_type=MESH)
    pl.semaphore_signal(barrier, inc=1, device_id={"pipe": nxt}, device_id_type=MESH)
    pl.semaphore_signal(barrier, inc=1, device_id={"pipe": prv}, device_id_type=MESH)

    cx = pltpu.make_async_copy(x_ref.at[0], xv, lsem.at[0])
    cg = pltpu.make_async_copy(g_ref, gv, lsem.at[1])
    cc = pltpu.make_async_copy(c_ref.at[0], cv, lsem.at[2])
    cx.start()
    cg.start()
    cws = [
        pltpu.make_async_copy(w_ref.at[0, pl.ds(k * KC, KC)], wv.at[pl.ds(k * KC, KC)], wsem.at[k])
        for k in range(NS)
    ]
    for cw in cws:
        cw.start()
    cc.start()

    pl.semaphore_wait(barrier, (nd - 1) + (nt - 1) + 2)

    xcp = []
    for k in range(NS):
        for o in range(1, nd):
            e = lax.rem(d + o, nd)
            cols = pl.ds(pl.multiple_of(e * K + k * KC, 128), KC)
            cp = remote(
                x_ref.at[0, :, cols], xr.at[o - 1, :, pl.ds(k * KC, KC)],
                x_s.at[o - 1, k], x_r.at[o - 1, k], dp=e,
            )
            cp.start()
            xcp.append(cp)

    cx.wait()
    ss = jnp.zeros((T, 1), F32)
    SC = D // 8
    for k in range(8):
        xf = xv[:, k * SC:(k + 1) * SC].astype(F32)
        ss = ss + jnp.sum(xf * xf, axis=-1, keepdims=True)
    scale = lax.rsqrt(ss * (1.0 / D) + 1e-05)
    rs[...] = jnp.broadcast_to(scale, rs.shape)
    stcp = []
    for o in range(1, nd):
        cp = remote(rs, rsr.at[o - 1], st_s.at[o - 1], st_r.at[o - 1], dp=lax.rem(d + o, nd))
        cp.start()
        stcp.append(cp)

    cg.wait()

    def gain(k):
        return gv[:, pl.ds(pl.multiple_of(d * K + k * KC, 128), KC)]

    for k in range(NS):
        xf = xv[:, pl.ds(pl.multiple_of(d * K + k * KC, 128), KC)].astype(F32)
        nb = (xf * rs[:, 0:1] * gain(k)).astype(BF16)
        cws[k].wait()
        part = jnp.dot(nb, wv[k * KC:(k + 1) * KC, :], preferred_element_type=F32)
        if k == 0:
            acc[0] = part
        else:
            acc[0] += part

    pcp = []
    for cp in stcp:
        cp.wait_recv()
    for k in range(NS):
        for o in range(1, nd):
            xcp[k * (nd - 1) + o - 1].wait_recv()
            xf = xr[o - 1, :, k * KC:(k + 1) * KC].astype(F32)
            nb = (xf * rsr[o - 1, :, 0:1] * gain(k)).astype(BF16)
            part = jnp.dot(nb, wv[k * KC:(k + 1) * KC, :], preferred_element_type=F32)
            if k == 0:
                acc[o] = part
            elif k < NS - 1:
                acc[o] += part
            else:
                ps[o - 1] = (acc[o] + part).astype(BF16)
                back = nd - o
                cp = remote(
                    ps.at[o - 1], pr.at[back - 1], p_s.at[back - 1], p_r.at[back - 1],
                    dp=lax.rem(d + back, nd),
                )
                cp.start()
                pcp.append(cp)
    for cp in pcp:
        cp.wait_recv()
    cc.wait()

    k0 = 0.7978845608028654
    k1 = 0.044715
    CB = 256
    for b in range(C // CB):
        cols = slice(b * CB, (b + 1) * CB)
        pre = acc[0, :, cols].astype(BF16).astype(F32)
        for o in range(1, nd):
            pre = pre + pr[o - 1, :, cols].astype(F32)
        sq = pre * pre
        th = jnp.tanh(k0 * (pre + k1 * (sq * pre)))
        cdf = 0.5 * (1.0 + th)
        slope = cdf + 0.5 * pre * ((1.0 - th * th) * (k0 * (1.0 + 3.0 * k1 * sq)))
        pgv[:, cols] = (cv[:, cols].astype(F32) * slope).astype(BF16)
        res = xv[:, pl.ds(pl.multiple_of(t * C + b * CB, 128), CB)].astype(F32)
        lo[:, cols] = (res + pre * cdf).astype(BF16)
    gcp = []
    for o in range(1, nd):
        cp = remote(pgv, pgr.at[o - 1], g_s.at[o - 1], g_r.at[o - 1], dp=lax.rem(d + o, nd))
        cp.start()
        gcp.append(cp)
    shcp = remote(lo, sh_ref.at[0], sh_s, sh_r, pipe=nxt)
    shcp.start()

    low = t < 2
    inner = jnp.where(low, 1, 2)
    outer = jnp.where(low, 0, 3)
    is_outer = t == outer
    is_inner = t == inner
    partner = inner + outer - t
    dests = [3 - outer, 3 - inner, partner, t]
    acp, rcp, ccp = [], [], []
    for s in range(nd):
        acp.append(remote(gp.at[s, 2], rb.at[s, 0], a_s.at[s], a_r.at[s], tensor=partner))
        rcp.append([remote(gp.at[s, j], rb.at[s, 2 + j], r_s.at[s, j], r_r.at[s, j], tensor=partner) for j in range(2)])
        ccp.append([remote(gp.at[s, j], rb.at[s, 1], c_s.at[s, j], c_r.at[s], tensor=dests[j]) for j in range(2)])
    for s in range(nd):
        if s:
            gcp[s - 1].wait_recv()
        for j in range(4):
            pg = pgr[s - 1] if s else pgv[...]
            wb = wv[pl.ds(pl.multiple_of(dests[j] * KQ, KQ), KQ), :]
            part = lax.dot_general(pg, wb, (((1,), (1,)), ((), ())), preferred_element_type=F32)
            gp[s, j] = part.astype(BF16)
            if j < 2:
                @pl.when(is_outer)
                def _():
                    rcp[s][j].start()
            elif j == 2:
                acp[s].start()

    @pl.when(is_inner)
    def _():
        for s in range(nd):
            for j in range(2):
                rcp[s][j].wait_recv()
                gp[s, j] = (gp[s, j].astype(F32) + rb[s, 2 + j].astype(F32)).astype(BF16)
                ccp[s][j].start()

    for s in range(nd):
        acp[s].wait_recv()
        ccp[s][0].wait_recv()
        src = lax.rem(d - s + nd, nd)
        ng_ref[0, pl.ds(pl.multiple_of(src * T, T), T), :] = (
            gp[s, 3].astype(F32) + rb[s, 0].astype(F32) + rb[s, 1].astype(F32)
        ).astype(BF16)

    for cp in xcp + stcp + pcp + gcp + acp:
        cp.wait_send()
    shcp.wait()

    @pl.when(is_outer)
    def _():
        for s in range(nd):
            for j in range(2):
                rcp[s][j].wait_send()

    @pl.when(is_inner)
    def _():
        for s in range(nd):
            for j in range(2):
                ccp[s][j].wait_send()


def per_device(np_, nd, nt, x, g, w, c):
    T, D = x.shape[1:]
    K, C = w.shape[1:]
    KQ = K // nt
    o = nd - 1
    dma = pltpu.SemaphoreType.DMA
    scratch = [
        pltpu.VMEM((T, D), BF16),
        pltpu.VMEM((1, D), F32),
        pltpu.VMEM((K, C), BF16),
        pltpu.VMEM((T, C), BF16),
        pltpu.VMEM((T, 128), F32),
        pltpu.VMEM((o, T, 128), F32),
        pltpu.VMEM((o, T, K), BF16),
        pltpu.VMEM((nd, T, C), F32),
        pltpu.VMEM((o, T, C), BF16),
        pltpu.VMEM((o, T, C), BF16),
        pltpu.VMEM((T, C), BF16),
        pltpu.VMEM((T, C), BF16),
        pltpu.VMEM((o, T, C), BF16),
        pltpu.VMEM((nd, 4, T, KQ), BF16),
        pltpu.VMEM((nd, 4, T, KQ), BF16),
        dma((3,)), dma((NS,)),
        dma((o,)), dma((o,)), dma((o, NS)), dma((o, NS)), dma((o,)), dma((o,)),
        dma((o,)), dma((o,)), dma, dma,
        dma((nd,)), dma((nd,)), dma((nd, 2)), dma((nd, 2)), dma((nd, 2)), dma((nd,)),
    ]
    hbm = pl.BlockSpec(memory_space=pl.ANY)
    return pl.pallas_call(
        functools.partial(kernel, np_, nd, nt),
        out_shape=(
            jax.ShapeDtypeStruct((1, T, C), BF16),
            jax.ShapeDtypeStruct((1, T * nd, KQ), BF16),
        ),
        in_specs=[hbm] * 4,
        out_specs=(hbm, pl.BlockSpec(memory_space=pltpu.VMEM)),
        scratch_shapes=scratch,
        compiler_params=pltpu.CompilerParams(
            collective_id=0, has_side_effects=True, vmem_limit_bytes=58 * 2**20
        ),
        cost_estimate=pl.CostEstimate(
            flops=4 * T * nd * K * C, bytes_accessed=2 * K * C + 4 * T * D, transcendentals=T * C
        ),
    )(x, g, w, c)


def solution(mesh):
    in_specs = (
        P("pipe", "dp", None),
        P("pipe", None),
        P("pipe", "dp", "tensor"),
        P("pipe", "dp", "tensor"),
    )
    out_specs = (P("pipe", "dp", "tensor"), P("pipe", None, ("dp", "tensor")))
    body = functools.partial(per_device, mesh.shape["pipe"], mesh.shape["dp"], mesh.shape["tensor"])
    return jax.shard_map(body, mesh=mesh, in_specs=in_specs, out_specs=out_specs, check_vma=False)
```

time: 98.7 us -> 50.2 us (0.51)
  Pallas kernels: 0 us -> 45.5 us
  waiting for transfers between devices: 39.3 us -> 0 us
  blocking collectives: 23.6 us -> 0 us
  between operations: 14.1 us -> 0.64 us
  matrix products: 12.7 us -> 0 us
  other arithmetic: 3.62 us -> 0 us
  local copies, waits for them, and re-layouts: 5 us -> 3.24 us
    pallas_call x0 -> x1, Pallas kernels: none -> 45.5 us  [per_device(): pl.pallas_call(functools.partial(kernel, np_, nd, nt), out_shape=(jax.Sha...]
    reduce_scatter x2 -> x0, waiting for transfers between devices: 34.9 us -> none  [the longest x1 22.8 us: per_device(): lax.psum_scatter(partial_grad.astype(jnp.bfloat16), 'tensor', scatter_dim...]
    all_to_all x1 -> x0, blocking collectives: 17.6 us -> none  [per_device(): lax.all_to_all(normed, 'dp', split_axis=1, concat_axis=0, tiled=True)]
    dot_general x2 -> x0, matrix products: 12.7 us -> none  [the longest x1 7.26 us: per_device(): lax.dot_general(grad_all, weight, (((1,), (1,)), ((), ())), preferred_ele...]
    all_gather x1 -> x0, blocking collectives: 5.93 us -> none  [per_device(): grad_all = lax.all_gather(pre_grad, 'dp', axis=0, tiled=True)]
    ppermute x1 -> x0, waiting for transfers between devices: 4.38 us -> none  [passed_along(): return lax.ppermute(block, axis, route)]
    convert_element_type x2 -> x0, local copies, waits for them, and re-layouts: 3.79 us -> none  [the longest x1 3.21 us: per_device(): xf = section_x.astype(jnp.float32)]
    convert_element_type x3 -> x0, other arithmetic: 2.59 us -> none  [the longest x1 1.33 us: per_device(): (xf * lax.rsqrt(meansq + 1e-05) * norm_gain[0]).astype(jnp.bfloat16)]
  transfers between devices with their start and end apart: 3 -> 0, of which waited for: 3 -> 0; matrix products, arithmetic and copies ran while one was open for 0% -> 0% of each run, Pallas kernels for 0% -> 0%
where the time goes in v1:
time: 50.2 us; the launch traced here: 49.4 us
  Pallas kernels  45.5 us (91%)
  local copies, waits for them, and re-layouts  3.24 us (6%)
  between operations  0.64 us (1%)
    pallas_call x1, Pallas kernels, per_device(): pl.pallas_call(functools.partial(kernel, np_, nd, nt), out_shape=(jax.Sha...  45.5 us
    unnamed x2, local copies, waits for them, and re-layouts  3.24 us

profile of v1, /device:TPU:0, one launch (start us, length us, event | category | flops | bytes accessed | tf_op | source)
XLA Modules:
  0.0 49.4 jit_solution(7065457559576083797)
XLA Ops:
  0.6 45.5 %shard_map.59 = (bf16[1,64,1024]{2,1,0:T(8,128)(2,1)}, bf16[1,128,1024]{2,1,0:T(8,128)(2,1)}) custom-call(bf16[1,64,8192]{2,1,0:T(8,128)(2,1)} %x_ref.1, f32[1,8192]{1,0:T(1,128)} %g_ref.1, bf16[1,4096,1024]{2,1,0:T(8,128)(2,1)} %w_ref.1, bf16[1,64,1024]{2,1,0:T(8,128)(2,1)} %c_ref.1), custom_call_target="tpu_custom_call" | custom-call | flops 2147483648 | bytes 10485760 | tf_op jit(solution)/shard_map/pallas_call | solution.py:240
  46.2 1.6 %copy.8 = bf16[1,64,1024]{2,1,0:T(8,128)(2,1)} copy(bf16[1,64,1024]{2,1,0:T(8,128)(2,1)} %get-tuple-element.4) | data formatting | bytes 262144
  47.8 1.7 %copy.9 = bf16[1,128,1024]{2,1,0:T(8,128)(2,1)} copy(bf16[1,128,1024]{2,1,0:T(8,128)(2,1)} %get-tuple-element.5) | data formatting | bytes 524288

commit v2 on v1

v2 whole, which is shorter than its diff:
```python
import functools

import jax
import jax.numpy as jnp
from jax import lax
from jax.experimental import pallas as pl
from jax.experimental.pallas import tpu as pltpu
from jax.sharding import PartitionSpec as P

F32 = jnp.float32
BF16 = jnp.bfloat16
MESH = pl.DeviceIdType.MESH
NB = 2
NS = 4


def kernel(
    np_, nd, nt,
    x_ref, g_ref, w_ref, c_ref,
    sh_ref, ng_ref,
    xv, gv, wv, cv, rs, rsr, xr, acc, ps, pr, lo, pgv, gp, rb,
    lsem, wsem,
    st_s, st_r, x_s, x_r, p_s, p_r, g_s, g_r, sh_s, sh_r,
    a_s, a_r, r_s, r_r, c_s, c_r,
):
    p = lax.axis_index("pipe")
    d = lax.axis_index("dp")
    t = lax.axis_index("tensor")
    T, D = x_ref.shape[1], x_ref.shape[2]
    K, C = w_ref.shape[1], w_ref.shape[2]
    KC, KQ, TB = K // NS, K // nt, T // NB

    def remote(src, dst, ss, rsem, **dev):
        return pltpu.make_async_remote_copy(
            src_ref=src, dst_ref=dst, send_sem=ss, recv_sem=rsem,
            device_id=dev, device_id_type=MESH,
        )

    nxt, prv = lax.rem(p + 1, np_), lax.rem(p + np_ - 1, np_)
    barrier = pltpu.get_barrier_semaphore()
    for o in range(1, nd):
        pl.semaphore_signal(barrier, inc=1, device_id={"dp": lax.rem(d + o, nd)}, device_id_type=MESH)
    for o in range(1, nt):
        pl.semaphore_signal(barrier, inc=1, device_id={"tensor": lax.rem(t + o, nt)}, device_id_type=MESH)
    pl.semaphore_signal(barrier, inc=1, device_id={"pipe": nxt}, device_id_type=MESH)
    pl.semaphore_signal(barrier, inc=1, device_id={"pipe": prv}, device_id_type=MESH)

    cx = pltpu.make_async_copy(x_ref.at[0], xv, lsem.at[0])
    cg = pltpu.make_async_copy(g_ref, gv, lsem.at[1])
    cc = pltpu.make_async_copy(c_ref.at[0], cv, lsem.at[2])
    cx.start()
    cg.start()
    cws = [
        pltpu.make_async_copy(w_ref.at[0, pl.ds(k * KC, KC)], wv.at[pl.ds(k * KC, KC)], wsem.at[k])
        for k in range(NS)
    ]
    for cw in cws:
        cw.start()
    cc.start()

    def peer(o):
        return lax.rem(d + o, nd)

    xcp = [[[
        remote(
            x_ref.at[0, pl.ds(b * TB, TB), pl.ds(pl.multiple_of(peer(o) * K + k * KC, 128), KC)],
            xr.at[o - 1, pl.ds(b * TB, TB), pl.ds(k * KC, KC)],
            x_s.at[b, o - 1, k], x_r.at[b, o - 1, k], dp=peer(o),
        ) for o in range(1, nd)] for k in range(NS)] for b in range(NB)]
    stcp = [
        remote(rs, rsr.at[o - 1], st_s.at[o - 1], st_r.at[o - 1], dp=peer(o)) for o in range(1, nd)
    ]
    pcp = [[
        remote(
            ps.at[b, nd - o - 1], pr.at[b, o - 1], p_s.at[b, o - 1], p_r.at[b, o - 1], dp=peer(o)
        ) for o in range(1, nd)] for b in range(NB)]
    gcp = [[
        remote(
            pgv.at[b, 0], pgv.at[b, o], g_s.at[b, o - 1], g_r.at[b, o - 1], dp=peer(o)
        ) for o in range(1, nd)] for b in range(NB)]
    shcp = [
        remote(lo.at[b], sh_ref.at[0, pl.ds(b * TB, TB)], sh_s.at[b], sh_r.at[b], pipe=nxt)
        for b in range(NB)
    ]

    def start_x(b, ks):
        for k in ks:
            for cp in xcp[b][k]:
                cp.start()

    pl.semaphore_wait(barrier, (nd - 1) + (nt - 1) + 2)

    start_x(0, range(NS))

    cx.wait()
    ss = jnp.zeros((T, 1), F32)
    SC = D // 8
    for k in range(8):
        xf = xv[:, k * SC:(k + 1) * SC].astype(F32)
        ss = ss + jnp.sum(xf * xf, axis=-1, keepdims=True)
    scale = lax.rsqrt(ss * (1.0 / D) + 1e-05)
    rs[...] = jnp.broadcast_to(scale, rs.shape)
    for cp in stcp:
        cp.start()
    start_x(1, range(1))

    cg.wait()

    def gain(k):
        return gv[:, pl.ds(pl.multiple_of(d * K + k * KC, 128), KC)]

    for k in range(NS):
        xf = xv[:, pl.ds(pl.multiple_of(d * K + k * KC, 128), KC)].astype(F32)
        nb = (xf * rs[:, 0:1] * gain(k)).astype(BF16)
        cws[k].wait()
        part = jnp.dot(nb, wv[k * KC:(k + 1) * KC, :], preferred_element_type=F32)
        if k == 0:
            acc[0] = part
        else:
            acc[0] += part
    for cp in stcp:
        cp.wait_recv()
    cc.wait()

    def project_peers(b):
        rows = slice(b * TB, (b + 1) * TB)
        for k in range(NS):
            for o in range(1, nd):
                xcp[b][k][o - 1].wait_recv()
                xf = xr[o - 1, rows, k * KC:(k + 1) * KC].astype(F32)
                nb = (xf * rsr[o - 1, rows, 0:1] * gain(k)).astype(BF16)
                part = jnp.dot(nb, wv[k * KC:(k + 1) * KC, :], preferred_element_type=F32)
                if k == 0:
                    acc[o, rows] = part
                elif k < NS - 1:
                    acc[o, rows] += part
                else:
                    ps[b, o - 1] = (acc[o, rows] + part).astype(BF16)
                    pcp[b][nd - o - 1].start()

    k0 = 0.7978845608028654
    k1 = 0.044715
    CB = 256

    def activate(b):
        rows = slice(b * TB, (b + 1) * TB)
        for cp in pcp[b]:
            cp.wait_recv()
        for i in range(C // CB):
            cols = slice(i * CB, (i + 1) * CB)
            pre = acc[0, rows, cols].astype(BF16).astype(F32)
            for o in range(1, nd):
                pre = pre + pr[b, o - 1, :, cols].astype(F32)
            sq = pre * pre
            th = jnp.tanh(k0 * (pre + k1 * (sq * pre)))
            cdf = 0.5 * (1.0 + th)
            slope = cdf + 0.5 * pre * ((1.0 - th * th) * (k0 * (1.0 + 3.0 * k1 * sq)))
            pgv[b, 0, :, cols] = (cv[rows, cols].astype(F32) * slope).astype(BF16)
            res = xv[rows, pl.ds(pl.multiple_of(t * C + i * CB, 128), CB)].astype(F32)
            lo[b, :, cols] = (res + pre * cdf).astype(BF16)
        for cp in gcp[b]:
            cp.start()
        shcp[b].start()

    low = t < 2
    inner = jnp.where(low, 1, 2)
    outer = jnp.where(low, 0, 3)
    is_outer = t == outer
    is_inner = t == inner
    partner = inner + outer - t
    dests = [3 - outer, 3 - inner, partner, t]
    acp, rcp, ccp = [], [], []
    for s in range(NB):
        acp.append(remote(gp.at[s, 2], rb.at[s, 0], a_s.at[s], a_r.at[s], tensor=partner))
        rcp.append([remote(gp.at[s, j], rb.at[s, 2 + j], r_s.at[s, j], r_r.at[s, j], tensor=partner) for j in range(2)])
        ccp.append([remote(gp.at[s, j], rb.at[s, 1], c_s.at[s, j], c_r.at[s], tensor=dests[j]) for j in range(2)])

    def input_grad(b):
        for cp in gcp[b]:
            cp.wait_recv()
        for j in range(4):
            pg = pgv[b].reshape(nd * TB, C)
            wb = wv[pl.ds(pl.multiple_of(dests[j] * KQ, KQ), KQ), :]
            part = lax.dot_general(pg, wb, (((1,), (1,)), ((), ())), preferred_element_type=F32)
            gp[b, j] = part.astype(BF16)
            if j < 2:
                @pl.when(is_outer)
                def _():
                    rcp[b][j].start()
            elif j == 2:
                acp[b].start()

    def relay(b, j):
        @pl.when(is_inner)
        def _():
            rcp[b][j].wait_recv()
            gp[b, j] = (gp[b, j].astype(F32) + rb[b, 2 + j].astype(F32)).astype(BF16)
            ccp[b][j].start()

    def finish(b):
        acp[b].wait_recv()
        ccp[b][0].wait_recv()
        for o in range(nd):
            r = slice(o * TB, (o + 1) * TB)
            row = pl.multiple_of(lax.rem(d - o + nd, nd) * T + b * TB, TB)
            ng_ref[0, pl.ds(row, TB), :] = (
                gp[b, 3, r].astype(F32) + rb[b, 0, r].astype(F32) + rb[b, 1, r].astype(F32)
            ).astype(BF16)

    project_peers(0)
    start_x(1, range(1, 3))
    activate(0)
    start_x(1, range(3, NS))
    input_grad(0)
    project_peers(1)
    relay(0, 0)
    activate(1)
    relay(0, 1)
    input_grad(1)
    relay(1, 0)
    relay(1, 1)
    finish(0)
    finish(1)

    for b in range(NB):
        for k in range(NS):
            for cp in xcp[b][k]:
                cp.wait_send()
        for cp in pcp[b] + gcp[b]:
            cp.wait_send()
        acp[b].wait_send()
        shcp[b].wait()
    for cp in stcp:
        cp.wait_send()

    @pl.when(is_outer)
    def _():
        for s in range(NB):
            for j in range(2):
                rcp[s][j].wait_send()

    @pl.when(is_inner)
    def _():
        for s in range(NB):
            for j in range(2):
                ccp[s][j].wait_send()


def place(a_ref, b_ref, oa_ref, ob_ref, sem):
    one = pltpu.make_async_copy(a_ref, oa_ref, sem.at[0])
    two = pltpu.make_async_copy(b_ref, ob_ref, sem.at[1])
    one.start()
    two.start()
    one.wait()
    two.wait()


def per_device(np_, nd, nt, x, g, w, c):
    T, D = x.shape[1:]
    K, C = w.shape[1:]
    KQ, TB = K // nt, T // NB
    o = nd - 1
    dma = pltpu.SemaphoreType.DMA
    scratch = [
        pltpu.VMEM((T, D), BF16),
        pltpu.VMEM((1, D), F32),
        pltpu.VMEM((K, C), BF16),
        pltpu.VMEM((T, C), BF16),
        pltpu.VMEM((T, 128), F32),
        pltpu.VMEM((o, T, 128), F32),
        pltpu.VMEM((o, T, K), BF16),
        pltpu.VMEM((nd, T, C), F32),
        pltpu.VMEM((NB, o, TB, C), BF16),
        pltpu.VMEM((NB, o, TB, C), BF16),
        pltpu.VMEM((NB, TB, C), BF16),
        pltpu.VMEM((NB, nd, TB, C), BF16),
        pltpu.VMEM((NB, 4, nd * TB, KQ), BF16),
        pltpu.VMEM((NB, 4, nd * TB, KQ), BF16),
        dma((3,)), dma((NS,)),
        dma((o,)), dma((o,)), dma((NB, o, NS)), dma((NB, o, NS)), dma((NB, o)), dma((NB, o)),
        dma((NB, o)), dma((NB, o)), dma((NB,)), dma((NB,)),
        dma((NB,)), dma((NB,)), dma((NB, 2)), dma((NB, 2)), dma((NB, 2)), dma((NB,)),
    ]
    hbm = pl.BlockSpec(memory_space=pl.ANY)
    shifted, grad = pl.pallas_call(
        functools.partial(kernel, np_, nd, nt),
        out_shape=(
            jax.ShapeDtypeStruct((1, T, C), BF16),
            jax.ShapeDtypeStruct((1, T * nd, KQ), BF16),
        ),
        in_specs=[hbm] * 4,
        out_specs=(hbm, pl.BlockSpec(memory_space=pltpu.VMEM)),
        scratch_shapes=scratch,
        compiler_params=pltpu.CompilerParams(
            collective_id=0, has_side_effects=True, vmem_limit_bytes=58 * 2**20
        ),
        cost_estimate=pl.CostEstimate(
            flops=4 * T * nd * K * C, bytes_accessed=2 * K * C + 4 * T * D, transcendentals=T * C
        ),
    )(x, g, w, c)
    return pl.pallas_call(
        place,
        out_shape=(
            jax.ShapeDtypeStruct(shifted.shape, BF16),
            jax.ShapeDtypeStruct(grad.shape, BF16),
        ),
        in_specs=[hbm] * 2,
        out_specs=(hbm, hbm),
        scratch_shapes=[dma((2,))],
    )(shifted, grad)


def solution(mesh):
    in_specs = (
        P("pipe", "dp", None),
        P("pipe", None),
        P("pipe", "dp", "tensor"),
        P("pipe", "dp", "tensor"),
    )
    out_specs = (P("pipe", "dp", "tensor"), P("pipe", None, ("dp", "tensor")))
    body = functools.partial(per_device, mesh.shape["pipe"], mesh.shape["dp"], mesh.shape["tensor"])
    return jax.shard_map(body, mesh=mesh, in_specs=in_specs, out_specs=out_specs, check_vma=False)
```

time: 50.2 us -> 59.5 us (1.19); the launches traced: 49.4 us -> 59.4 us
  Pallas kernels: 45.5 us -> 58.8 us
  local copies, waits for them, and re-layouts: 3.24 us -> 0 us
    pallas_call x0 -> x1, Pallas kernels: none -> 13 us  [per_device(): pl.pallas_call(place, out_shape=(jax.ShapeDtypeStruct(shifted.shape, BF16...]
    unnamed x2 -> x0, local copies, waits for them, and re-layouts: 3.24 us -> none
where the time goes in v2:
time: 59.5 us; the launch traced here: 59.4 us
  Pallas kernels  58.8 us (99%)
  between operations  0.64 us (1%)
    pallas_call x1, Pallas kernels, per_device(): pl.pallas_call(functools.partial(kernel, np_, nd, nt), out_shape=(jax.Sha...  45.7 us
    pallas_call x1, Pallas kernels, per_device(): pl.pallas_call(place, out_shape=(jax.ShapeDtypeStruct(shifted.shape, BF16...  13 us

profile of v2, /device:TPU:0, one launch (start us, length us, event | category | flops | bytes accessed | tf_op | source)
XLA Modules:
  0.0 59.4 jit_solution(16679878011204814896)
XLA Ops:
  0.6 45.7 %shard_map.59 = (bf16[1,64,1024]{2,1,0:T(8,128)(2,1)}, bf16[1,128,1024]{2,1,0:T(8,128)(2,1)}) custom-call(bf16[1,64,8192]{2,1,0:T(8,128)(2,1)} %x_ref.1, f32[1,8192]{1,0:T(1,128)} %g_ref.1, bf16[1,4096,1024]{2,1,0:T(8,128)(2,1)} %w_ref.1, bf16[1,64,1024]{2,1,0:T(8,128)(2,1)} %c_ref.1), custom_call_target="tpu_custom_call" | custom-call | flops 2147483648 | bytes 10485760 | tf_op jit(solution)/shard_map/pallas_call | solution.py:285
  46.4 13.0 %shard_map.60 = (bf16[1,64,1024]{2,1,0:T(8,128)(2,1)}, bf16[1,128,1024]{2,1,0:T(8,128)(2,1)}) custom-call(bf16[1,64,1024]{2,1,0:T(8,128)(2,1)} %get-tuple-element.4.a_ref, bf16[1,128,1024]{2,1,0:T(8,128)(2,1)} %get-tuple-element.5.b_ref), custom_call_target="tpu_custom_call" | custom-call | tf_op jit(solution)/shard_map/pallas_call | solution.py:301

commit v3 on v2

--- a/solution.py
+++ b/solution.py
@@ -102,7 +102,7 @@
     rs[...] = jnp.broadcast_to(scale, rs.shape)
     for cp in stcp:
         cp.start()
-    start_x(1, range(1))
+    start_x(1, range(2))
 
     cg.wait()
 
@@ -208,13 +208,12 @@
             ).astype(BF16)
 
     project_peers(0)
-    start_x(1, range(1, 3))
+    start_x(1, range(2, NS))
     activate(0)
-    start_x(1, range(3, NS))
+    project_peers(1)
     input_grad(0)
-    project_peers(1)
+    activate(1)
     relay(0, 0)
-    activate(1)
     relay(0, 1)
     input_grad(1)
     relay(1, 0)
@@ -246,13 +245,9 @@
                 ccp[s][j].wait_send()
 
 
-def place(a_ref, b_ref, oa_ref, ob_ref, sem):
-    one = pltpu.make_async_copy(a_ref, oa_ref, sem.at[0])
-    two = pltpu.make_async_copy(b_ref, ob_ref, sem.at[1])
-    one.start()
-    two.start()
-    one.wait()
-    two.wait()
+def place(a_ref, b_ref, oa_ref, ob_ref):
+    oa_ref[...] = a_ref[...]
+    ob_ref[...] = b_ref[...]
 
 
 def per_device(np_, nd, nt, x, g, w, c):
@@ -281,6 +276,7 @@
         dma((NB, o)), dma((NB, o)), dma((NB,)), dma((NB,)),
         dma((NB,)), dma((NB,)), dma((NB, 2)), dma((NB, 2)), dma((NB, 2)), dma((NB,)),
     ]
+    vmem = pl.BlockSpec(memory_space=pltpu.VMEM)
     hbm = pl.BlockSpec(memory_space=pl.ANY)
     shifted, grad = pl.pallas_call(
         functools.partial(kernel, np_, nd, nt),
@@ -304,9 +300,8 @@
             jax.ShapeDtypeStruct(shifted.shape, BF16),
             jax.ShapeDtypeStruct(grad.shape, BF16),
         ),
-        in_specs=[hbm] * 2,
-        out_specs=(hbm, hbm),
-        scratch_shapes=[dma((2,))],
+        in_specs=[vmem] * 2,
+        out_specs=(vmem, vmem),
     )(shifted, grad)
 
 

time: 59.5 us -> 46 us (0.77)
  Pallas kernels: 58.8 us -> 45.1 us
    pallas_call x1, Pallas kernels: 13 us -> 1.78 us  [per_device(): pl.pallas_call(place, out_shape=(jax.ShapeDtypeStruct(shifted.shape, BF16...]
    pallas_call x1, Pallas kernels: 45.7 us -> 43.3 us  [per_device(): pl.pallas_call(functools.partial(kernel, np_, nd, nt), out_shape=(jax.Sha...]
where the time goes in v3:
time: 46 us; the launch traced here: 45.7 us
  Pallas kernels  45.1 us (98%)
  between operations  0.64 us (1%)
    pallas_call x1, Pallas kernels, per_device(): pl.pallas_call(functools.partial(kernel, np_, nd, nt), out_shape=(jax.Sha...  43.3 us
    pallas_call x1, Pallas kernels, per_device(): pl.pallas_call(place, out_shape=(jax.ShapeDtypeStruct(shifted.shape, BF16...  1.78 us

profile of v3, /device:TPU:0, one launch (start us, length us, event | category | flops | bytes accessed | tf_op | source)
XLA Modules:
  0.0 45.7 jit_solution(17557148213192053812)
XLA Ops:
  0.6 43.3 %shard_map.59 = (bf16[1,64,1024]{2,1,0:T(8,128)(2,1)}, bf16[1,128,1024]{2,1,0:T(8,128)(2,1)}) custom-call(bf16[1,64,8192]{2,1,0:T(8,128)(2,1)} %x_ref.1, f32[1,8192]{1,0:T(1,128)} %g_ref.1, bf16[1,4096,1024]{2,1,0:T(8,128)(2,1)} %w_ref.1, bf16[1,64,1024]{2,1,0:T(8,128)(2,1)} %c_ref.1), custom_call_target="tpu_custom_call" | custom-call | flops 2147483648 | bytes 10485760 | tf_op jit(solution)/shard_map/pallas_call | solution.py:281
  43.9 1.8 %shard_map.60 = (bf16[1,64,1024]{2,1,0:T(8,128)(2,1)}, bf16[1,128,1024]{2,1,0:T(8,128)(2,1)}) custom-call(bf16[1,64,1024]{2,1,0:T(8,128)(2,1)} %get-tuple-element.4.a_ref, bf16[1,128,1024]{2,1,0:T(8,128)(2,1)} %get-tuple-element.5.b_ref), custom_call_target="tpu_custom_call" | custom-call | tf_op jit(solution)/shard_map/pallas_call | solution.py:297

commit v4 on v3

--- a/solution.py
+++ b/solution.py
@@ -63,7 +63,7 @@
 
     xcp = [[[
         remote(
-            x_ref.at[0, pl.ds(b * TB, TB), pl.ds(pl.multiple_of(peer(o) * K + k * KC, 128), KC)],
+            xv.at[pl.ds(b * TB, TB), pl.ds(pl.multiple_of(peer(o) * K + k * KC, 128), KC)],
             xr.at[o - 1, pl.ds(b * TB, TB), pl.ds(k * KC, KC)],
             x_s.at[b, o - 1, k], x_r.at[b, o - 1, k], dp=peer(o),
         ) for o in range(1, nd)] for k in range(NS)] for b in range(NB)]
@@ -88,10 +88,6 @@
             for cp in xcp[b][k]:
                 cp.start()
 
-    pl.semaphore_wait(barrier, (nd - 1) + (nt - 1) + 2)
-
-    start_x(0, range(NS))
-
     cx.wait()
     ss = jnp.zeros((T, 1), F32)
     SC = D // 8
@@ -100,6 +96,10 @@
         ss = ss + jnp.sum(xf * xf, axis=-1, keepdims=True)
     scale = lax.rsqrt(ss * (1.0 / D) + 1e-05)
     rs[...] = jnp.broadcast_to(scale, rs.shape)
+
+    pl.semaphore_wait(barrier, (nd - 1) + (nt - 1) + 2)
+
+    start_x(0, range(NS))
     for cp in stcp:
         cp.start()
     start_x(1, range(2))

time: 46 us -> 45.3 us (0.985)
  Pallas kernels: 45.1 us -> 44.5 us
    pallas_call x1, Pallas kernels: 43.3 us -> 42.7 us  [per_device(): pl.pallas_call(functools.partial(kernel, np_, nd, nt), out_shape=(jax.Sha...]
where the time goes in v4:
time: 45.3 us; the launch traced here: 45.1 us
  Pallas kernels  44.5 us (98%)
  between operations  0.64 us (1%)
    pallas_call x1, Pallas kernels, per_device(): pl.pallas_call(functools.partial(kernel, np_, nd, nt), out_shape=(jax.Sha...  42.7 us
    pallas_call x1, Pallas kernels, per_device(): pl.pallas_call(place, out_shape=(jax.ShapeDtypeStruct(shifted.shape, BF16...  1.78 us

profile of v4, /device:TPU:0, one launch (start us, length us, event | category | flops | bytes accessed | tf_op | source)
XLA Modules:
  0.0 45.1 jit_solution(994433183272659821)
XLA Ops:
  0.6 42.7 %shard_map.59 = (bf16[1,64,1024]{2,1,0:T(8,128)(2,1)}, bf16[1,128,1024]{2,1,0:T(8,128)(2,1)}) custom-call(bf16[1,64,8192]{2,1,0:T(8,128)(2,1)} %x_ref.1, f32[1,8192]{1,0:T(1,128)} %g_ref.1, bf16[1,4096,1024]{2,1,0:T(8,128)(2,1)} %w_ref.1, bf16[1,64,1024]{2,1,0:T(8,128)(2,1)} %c_ref.1), custom_call_target="tpu_custom_call" | custom-call | flops 2147483648 | bytes 10485760 | tf_op jit(solution)/shard_map/pallas_call | solution.py:281
  43.3 1.8 %shard_map.60 = (bf16[1,64,1024]{2,1,0:T(8,128)(2,1)}, bf16[1,128,1024]{2,1,0:T(8,128)(2,1)}) custom-call(bf16[1,64,1024]{2,1,0:T(8,128)(2,1)} %get-tuple-element.4.a_ref, bf16[1,128,1024]{2,1,0:T(8,128)(2,1)} %get-tuple-element.5.b_ref), custom_call_target="tpu_custom_call" | custom-call | tf_op jit(solution)/shard_map/pallas_call | solution.py:297

commit v5 on v4

--- a/solution.py
+++ b/solution.py
@@ -214,8 +214,8 @@
     input_grad(0)
     activate(1)
     relay(0, 0)
+    input_grad(1)
     relay(0, 1)
-    input_grad(1)
     relay(1, 0)
     relay(1, 1)
     finish(0)

time: 45.3 us -> 45.3 us (level)
  no operation moved by 1% of the time
where the time goes in v5:
time: 45.3 us; the launch traced here: 45.1 us
  Pallas kernels  44.5 us (98%)
  between operations  0.64 us (1%)
    pallas_call x1, Pallas kernels, per_device(): pl.pallas_call(functools.partial(kernel, np_, nd, nt), out_shape=(jax.Sha...  42.7 us
    pallas_call x1, Pallas kernels, per_device(): pl.pallas_call(place, out_shape=(jax.ShapeDtypeStruct(shifted.shape, BF16...  1.78 us

profile of v5, /device:TPU:0, one launch (start us, length us, event | category | flops | bytes accessed | tf_op | source)
XLA Modules:
  0.0 45.1 jit_solution(13207882032899169126)
XLA Ops:
  0.6 42.7 %shard_map.59 = (bf16[1,64,1024]{2,1,0:T(8,128)(2,1)}, bf16[1,128,1024]{2,1,0:T(8,128)(2,1)}) custom-call(bf16[1,64,8192]{2,1,0:T(8,128)(2,1)} %x_ref.1, f32[1,8192]{1,0:T(1,128)} %g_ref.1, bf16[1,4096,1024]{2,1,0:T(8,128)(2,1)} %w_ref.1, bf16[1,64,1024]{2,1,0:T(8,128)(2,1)} %c_ref.1), custom_call_target="tpu_custom_call" | custom-call | flops 2147483648 | bytes 10485760 | tf_op jit(solution)/shard_map/pallas_call | solution.py:281
  43.3 1.8 %shard_map.60 = (bf16[1,64,1024]{2,1,0:T(8,128)(2,1)}, bf16[1,128,1024]{2,1,0:T(8,128)(2,1)}) custom-call(bf16[1,64,1024]{2,1,0:T(8,128)(2,1)} %get-tuple-element.4.a_ref, bf16[1,128,1024]{2,1,0:T(8,128)(2,1)} %get-tuple-element.5.b_ref), custom_call_target="tpu_custom_call" | custom-call | tf_op jit(solution)/shard_map/pallas_call | solution.py:297
